TPU v7x, 128 devices: a whole 4x4x4 slice. The times are simulated.
128 devices in a mesh: half: 2 (over z_hi), row: 8 (over x, core), col: 8 (over z_lo, y).
Axes of the slice: x: 4, y: 4, z: 4 (z_hi: 2, z_lo: 2; z = z_hi * 2 + z_lo), core: 2. Of those that a mesh axis runs over, the one named last changes fastest.
Arguments:
- front: bfloat16 [2, 16384, 16384], P('half', 'row', 'col'), may hold values from -6 to 6, as said below
- panel: bfloat16 [2, 16384, 1024], P('half', 'row', 'col'), may hold values from -2.5 to 2.5
- inverse_block: bfloat16 [2, 1024, 1024], P('half', None, 'col'), as said below
- child_maps: int32 [2, 16384], replicated, may hold values from 0 to 16383, as said below
- root_front: bfloat16 [16384, 16384], P(('half', 'row'), 'col'), may hold values from -6 to 6, as said below
Outputs:
- root_sum: float32 [16384, 16384], P(('half', 'row'), 'col')
Inputs may be any that keep to these rules, and one draw needn't show every extreme that they name: `child_maps`: each row is a permutation of the 16384 root indices. For each child, in every aligned block of 2048 positions, the k-th aligned run of 128 positions maps into the k-th aligned block of 1024 root indices. `inverse_block`: each matrix is lower triangular with a positive diagonal. `front`: each child's matrix is symmetric. `root_front`: the matrix is symmetric.
All inputs are finite; a program needn't handle non-finite values.
Results may differ from a plain program's by a relative error of at most 0.0041.
Values may be sent and summed in bfloat16 or wider, within the bound.
No kernel may reach another device: no remote copies, remote signals or barrier semaphores. Data moves between devices by JAX's collectives and lax.ppermute only.
A program may use at most 128 MiB of HBM per device.

v0:
```python
import functools

import jax
import jax.numpy as jnp
from jax import lax
from jax.experimental import pallas as pl
from jax.experimental.pallas import tpu as pltpu
from jax.sharding import PartitionSpec as P

ALL = ("half", "row", "col")
BF16 = jnp.bfloat16
F32 = jnp.float32
VMEM_LIMIT = 58 * 1024 * 1024


def device_pairs(move):
    pairs = []
    for half in range(2):
        for row in range(8):
            for col in range(8):
                zh, x, core, zl, y = move(half, row // 2, row % 2, col // 4, col % 4)
                source = (half * 8 + row) * 8 + col
                pairs.append((source, (zh * 8 + 2 * x + core) * 8 + 4 * zl + y))
    return pairs


def shift(array, move):
    return lax.ppermute(array, ALL, device_pairs(move))


def ring(array, forward, backward):
    behind = shift(array, forward)
    ahead = shift(array, backward)
    far_first = shift(behind[0], forward)
    far_second = shift(ahead[1], backward)
    return array, behind, ahead, far_first, far_second


def lower_kernel(core_ref, panel_ref, mine_ref, other_ref, out_ref):
    core = core_ref[0]
    wide = mine_ref.shape[1]
    for ref, part in ((mine_ref, core), (other_ref, 1 - core)):
        total = jnp.zeros((panel_ref.shape[1], wide), F32)
        for chunk in range(panel_ref.shape[0]):
            total += lax.dot_general(
                panel_ref[chunk],
                ref[chunk],
                (((1,), (1,)), ((), ())),
                preferred_element_type=F32,
            )
        out_ref[:, pl.ds(pl.multiple_of(part * wide, wide), wide)] = total.astype(BF16)


def lower_piece(core, panel, mine, other):
    whole = pl.BlockSpec(memory_space=pltpu.VMEM)
    return pl.pallas_call(
        lower_kernel,
        out_shape=jax.ShapeDtypeStruct((panel.shape[1], 2 * mine.shape[1]), BF16),
        in_specs=[pl.BlockSpec(memory_space=pltpu.SMEM), whole, whole, whole],
        out_specs=whole,
        compiler_params=pltpu.CompilerParams(vmem_limit_bytes=VMEM_LIMIT),
        cost_estimate=pl.CostEstimate(
            flops=2 * 256 * 1024 * 1024, bytes_accessed=3 << 20, transcendentals=0
        ),
        name="lower",
    )(core, panel, mine, other)


def update_kernel(place_ref, *refs):
    rows, mine, other = refs[0:5], refs[5:10], refs[10:15]
    out_ref, left_ref, right_ref = refs[15:18]
    child = pl.program_id(0)
    x, core, y = place_ref[0], place_ref[1], place_ref[2]

    def gather(refs, base, store):
        near, behind, ahead, far_first, far_second = refs
        store(base, near[child])
        store((base + 3) % 4, behind[child])
        store((base + 1) % 4, ahead[child])

        @pl.when(child == 0)
        def _():
            store((base + 2) % 4, far_first[...])

        @pl.when(child == 1)
        def _():
            store((base + 2) % 4, far_second[...])

    def store_rows(at, value):
        left_ref[pl.ds(pl.multiple_of(at * 256, 256), 256), :] = value

    def store_cols(which):
        def store(at, value):
            block = (at * 2 + which) * 128
            for b in range(2):
                right_ref[b, pl.ds(pl.multiple_of(block, 128), 128), :] = value[
                    b * 128 : (b + 1) * 128
                ]

        return store

    gather(rows, y, store_rows)
    gather(mine, x, store_cols(core))
    gather(other, x, store_cols(1 - core))
    for b in range(2):
        for part in range(4):
            span = slice(part * 256, (part + 1) * 256)
            out_ref[0, b, span, :] = lax.dot_general(
                left_ref[span, :],
                right_ref[b],
                (((1,), (1,)), ((), ())),
                preferred_element_type=F32,
            )


def update(place, rows, mine, other):
    whole = pl.BlockSpec(memory_space=pltpu.VMEM)
    return pl.pallas_call(
        update_kernel,
        grid=(2,),
        out_shape=jax.ShapeDtypeStruct((2, 2, 1024, 1024), F32),
        in_specs=[pl.BlockSpec(memory_space=pltpu.SMEM)] + [whole] * 15,
        out_specs=pl.BlockSpec((1, 2, 1024, 1024), lambda c: (c, 0, 0, 0)),
        scratch_shapes=[
            pltpu.VMEM((1024, 1024), BF16),
            pltpu.VMEM((2, 1024, 1024), BF16),
        ],
        compiler_params=pltpu.CompilerParams(vmem_limit_bytes=VMEM_LIMIT),
        cost_estimate=pl.CostEstimate(
            flops=2 * 4 << 30, bytes_accessed=28 << 20, transcendentals=0
        ),
        name="update",
    )(place, *rows, *mine, *other)


ROWS_STEP = 256


def place_kernel(
    flip,
    last,
    place_ref,
    front_ref,
    update_ref,
    row_map_ref,
    col_map_ref,
    base_ref,
    out_ref,
    schur_ref,
    pick_ref,
):
    b, step = pl.program_id(0), pl.program_id(1)

    @pl.when(step == 0)
    def _():
        for r in range(8):
            for c in range(8):
                rows, cols = slice(r * 128, (r + 1) * 128), slice(c * 128, (c + 1) * 128)
                entry = front_ref[r * 8 + (c ^ flip)].astype(F32)
                schur_ref[rows, cols] = (entry - update_ref[0, 0, rows, cols]).astype(BF16)
        ids = lax.broadcasted_iota(jnp.int32, (1024, 1024), 1)
        pick_ref[...] = jnp.where(col_map_ref[0] == ids, 1.0, 0.0).astype(BF16)

    first = step * ROWS_STEP
    ids = lax.broadcasted_iota(jnp.int32, (ROWS_STEP, 1024), 0) + first
    row_pick = jnp.where(row_map_ref[...] == ids, 1.0, 0.0).astype(BF16)
    rowed = jnp.dot(row_pick, schur_ref[...], preferred_element_type=F32).astype(BF16)
    placed = jnp.dot(rowed, pick_ref[...], preferred_element_type=F32)
    total = base_ref[...].astype(F32) + placed
    if last:
        shape = (ROWS_STEP, 1024)
        row_ids = lax.broadcasted_iota(jnp.int32, shape, 0) + (place_ref[3] * 1024 + first)
        col_ids = lax.broadcasted_iota(jnp.int32, shape, 1) + (
            place_ref[4] * 2048 + b * 1024
        )
        total = jnp.where(row_ids >= col_ids, total, 0.0)
    out_ref[...] = total


def place_child(place, child, front, updates, row_map, col_map, base, flip, last):
    grid_spec = pltpu.PrefetchScalarGridSpec(
        num_scalar_prefetch=1,
        grid=(2, 1024 // ROWS_STEP),
        in_specs=[
            pl.BlockSpec((64, 128, 128), lambda b, i, s: (0, 0, b)),
            pl.BlockSpec((1, 1, 1024, 1024), lambda b, i, s: (s[child], b, 0, 0)),
            pl.BlockSpec((1, 1024), lambda b, i, s: (0, 0)),
            pl.BlockSpec((1, 1024, 1), lambda b, i, s: (b, 0, 0)),
            pl.BlockSpec((ROWS_STEP, 1024), lambda b, i, s: (i, b)),
        ],
        out_specs=pl.BlockSpec((ROWS_STEP, 1024), lambda b, i, s: (i, b)),
        scratch_shapes=[
            pltpu.VMEM((1024, 1024), BF16),
            pltpu.VMEM((1024, 1024), BF16),
        ],
    )
    return pl.pallas_call(
        functools.partial(place_kernel, flip, last),
        grid_spec=grid_spec,
        out_shape=jax.ShapeDtypeStruct((1024, 2048), F32),
        compiler_params=pltpu.CompilerParams(vmem_limit_bytes=VMEM_LIMIT),
        cost_estimate=pl.CostEstimate(
            flops=2 * 4 << 30, bytes_accessed=28 << 20, transcendentals=0
        ),
        name="place_last" if last else "place_first",
    )(place, front, updates, row_map, col_map, base)


def body(front, panel, inverse_block, child_maps, root_front):
    half = lax.axis_index("half")
    row = lax.axis_index("row")
    col = lax.axis_index("col")
    x, core, zl, y = row // 2, row % 2, col // 4, col % 4
    target = half * 8 + row

    parcels = front[0].reshape(2, 8, 128, 8, 256).transpose(0, 1, 3, 2, 4)
    stay = lax.dynamic_index_in_dim(parcels, half, 0, keepdims=False).reshape(64, 128, 256)
    leave = lax.dynamic_index_in_dim(parcels, 1 - half, 0, keepdims=False).reshape(
        64, 128, 256
    )
    crossed = shift(leave, lambda zh, x, k, zl, y: (1 - zh, x, k, 1 - zl, y))

    inverse_share = lax.dynamic_slice_in_dim(inverse_block[0], core * 512, 512, 0)
    packet = jnp.concatenate(
        [panel[0].reshape(8, 256, 128), jnp.broadcast_to(inverse_share, (8, 512, 128))], 1
    )
    packet = lax.all_to_all(packet, "col", 0, 0, tiled=True)
    own_inverse = packet[:, 256:]
    other_inverse = shift(own_inverse, lambda zh, x, k, zl, y: (zh, x, 1 - k, zl, y))
    piece = lower_piece(core.reshape(1), packet[:, :256], own_inverse, other_inverse)

    def ordered(first, second, swapped):
        return jnp.stack(
            [jnp.where(swapped, second, first), jnp.where(swapped, first, second)]
        )

    twin = shift(piece, lambda zh, x, k, zl, y: (1 - zh, x, k, zl, y))
    columns = ring(
        ordered(piece, twin, half == 1),
        lambda zh, x, k, zl, y: (zh, (x + 1) % 4, k, zl, y),
        lambda zh, x, k, zl, y: (zh, (x + 3) % 4, k, zl, y),
    )
    columns_other = [
        shift(part, lambda zh, x, k, zl, y: (zh, x, 1 - k, zl, y)) for part in columns
    ]

    same = shift(
        lax.dynamic_slice_in_dim(piece, core * 128, 128, 0),
        lambda zh, x, k, zl, y: (zl, y, k, zh, x),
    )
    cross = shift(
        lax.dynamic_slice_in_dim(piece, (1 - core) * 128, 128, 0),
        lambda zh, x, k, zl, y: (zl, y, 1 - k, zh, x),
    )
    strip = ordered(same, cross, core == 1).reshape(256, 1024)
    strip_twin = shift(strip, lambda zh, x, k, zl, y: (zh, x, k, 1 - zl, y))
    rows = ring(
        ordered(strip, strip_twin, zl == 1),
        lambda zh, x, k, zl, y: (zh, x, k, zl, (y + 1) % 4),
        lambda zh, x, k, zl, y: (zh, x, k, zl, (y + 3) % 4),
    )

    place = jnp.stack([x, core, y, target, col, half, 1 - half]).astype(jnp.int32)
    updates = update(place, rows, columns, columns_other)

    stayed = lax.all_to_all(stay, ("row", "col"), 0, 0, tiled=True)
    arrived = lax.all_to_all(crossed, ("row", "col"), 0, 0, tiled=True)

    maps = child_maps.reshape(2, 8, 16, 128)
    row_maps = (
        lax.dynamic_index_in_dim(maps, target, 2, keepdims=False).reshape(2, 1, 1024)
        - target * 1024
    )
    col_maps = lax.dynamic_slice_in_dim(maps, 2 * col, 2, 2).transpose(0, 2, 1, 3)
    col_maps = col_maps - (2 * col + jnp.arange(2, dtype=jnp.int32))[None, :, None, None] * 1024
    col_maps = col_maps.reshape(2, 2, 1024, 1)

    def pick(array, which):
        return lax.dynamic_index_in_dim(array, which, 0, keepdims=False)

    summed = place_child(
        place,
        5,
        stayed,
        updates,
        pick(row_maps, half),
        pick(col_maps, half),
        root_front,
        0,
        False,
    )
    return place_child(
        place,
        6,
        arrived,
        updates,
        pick(row_maps, 1 - half),
        pick(col_maps, 1 - half),
        summed,
        4,
        True,
    )


def solution(mesh):
    return jax.shard_map(
        body,
        mesh=mesh,
        in_specs=(
            P("half", "row", "col"),
            P("half", "row", "col"),
            P("half", None, "col"),
            P(),
            P(("half", "row"), "col"),
        ),
        out_specs=P(("half", "row"), "col"),
        check_vma=False,
    )
```

profile of v0, /device:TPU:1, one launch (start us, length us, event | category | flops | bytes accessed | tf_op | source)
XLA Modules:
  0.0 316.7 jit_solution(18002447968464273846)
XLA Ops:
  0.0 0.9 copy-done
  1.1 2.3 pad_maximum_fusion
  3.4 6.4 %all-to-all-start.1 = ((bf16[8,768,128]{2,1,0:T(8,128)(2,1)}), bf16[8,768,128]{2,1,0:T(8,128)(2,1)S(1)}, u32[]{:S(2)}, u32[]{:S(2)}) async-start(bf16[8,768,128]{2,1,0:T(8,128)(2,1)} %pad_maximum_fusion), calls=%async_computation.1 | async-start | bytes 3145728 | tf_op jit(solution)/shard_map/all_to_all | solution.py:227
  9.8 10.5 %copy.14 = bf16[256,8,8,256]{3,2,1,0:T(8,128)(2,1)} copy(bf16[256,8,8,256]{3,1,2,0:T(8,128)(2,1)} %bitcast.60) | data formatting | bytes 16777216
  20.3 4.0 %constant_dynamic-slice_fusion = (bf16[1,8,128,8,256]{4,3,2,1,0:T(8,128)(2,1)S(1)}, bf16[1,8,128,8,256]{4,3,2,1,0:T(8,128)(2,1)S(1)}) fusion(bf16[2,8,128,8,256]{4,3,2,1,0:T(8,128)(2,1)} %bitcast.58, s32[]{:T(128)S(6)} %select_n.100, s32[]{:T(128)S(6)} %select_n.84), kind=kLoop, calls=%fused_computation.21 | loop fusion | bytes 16777224 | tf_op jit(solution)/shard_map/dynamic-slice.2
  24.3 3.1 copy.12
  27.4 3.6 %collective-permute-start = (bf16[64,128,256]{2,1,0:T(8,128)(2,1)}, bf16[64,128,256]{2,1,0:T(8,128)(2,1)}, u32[]{:S(2)}, u32[]{:S(2)}) collective-permute-start(bf16[64,128,256]{2,1,0:T(8,128)(2,1)} %bitcast.8), channel_id=1, source_target_pairs={{0,68},{1,69},{2,70},{3,71},{4,64},{5,65},{6,66},{7,67},{8,76},{9,... | collective-permute-start | bytes 12582920 | tf_op jit(solution)/shard_map/ppermute | solution.py:28
  31.0 3.1 copy.13
  34.0 9.0 %all-to-all-start.2 = ((bf16[64,128,256]{2,1,0:T(8,128)(2,1)}), bf16[64,128,256]{2,1,0:T(8,128)(2,1)}, u32[]{:S(2)}, u32[]{:S(2)}) async-start(bf16[64,128,256]{2,1,0:T(8,128)(2,1)} %bitcast.59), calls=%async_computation.2 | async-start | bytes 8388608 | tf_op jit(solution)/shard_map/all_to_all | solution.py:266
  43.1 0.6 collective-permute-start.1
  43.7 0.8 slice.24.panel_ref
  44.6 1.6 collective-permute-done.1.other_ref
  46.1 3.7 %lower.1 = bf16[256,1024]{1,0:T(8,128)(2,1)} custom-call(s32[1]{0:T(128)} %bitcast.1.core_ref, bf16[8,256,128]{2,1,0:T(8,128)(2,1)} %slice.24.panel_ref, bf16[8,512,128]{2,1,0:T(8,128)(2,1)} %copy-done.2, bf16[8,512,128]{2,1,0:T(8,128)(2,1)} %collective-permute-done.1.other_ref), custom_call_target="tpu_custom_call" | custom-call | flops 536870912 | bytes 3145728 | tf_op jit(solution)/shard_map/lower/pallas_call | solution.py:56
  49.9 1.1 constant_dynamic-slice_fusion.2
  50.9 0.5 collective-permute-start.2
  51.4 0.7 collective-permute-start.3
  52.1 4.2 %collective-permute-start.9 = (bf16[256,1024]{1,0:T(8,128)(2,1)}, bf16[256,1024]{1,0:T(8,128)(2,1)S(1)}, u32[]{:S(2)}, u32[]{:S(2)}) collective-permute-start(bf16[256,1024]{1,0:T(8,128)(2,1)} %lower.1), channel_id=1, source_target_pairs={{0,64},{1,65},{2,66},{3,67},{4,68},{5,69},{6,70},{7,71},{8,72},{9,... | collective-permute-start | bytes 1572872 | tf_op jit(solution)/shard_map/ppermute | solution.py:28
  56.4 86.3 %collective-permute-start.4 = (bf16[256,1024]{1,0:T(8,128)(2,1)S(1)}, bf16[256,1024]{1,0:T(8,128)(2,1)S(1)}, u32[]{:S(2)}, u32[]{:S(2)}) collective-permute-start(bf16[256,1024]{1,0:T(8,128)(2,1)S(1)} %bitcast.61), channel_id=1, source_target_pairs={{0,4},{1,5},{2,6},{3,7},{4,0},{5,1},{6,2},{7,3},{8,12},{9,13},{10,... | collective-permute-start | bytes 1572872 | tf_op jit(solution)/shard_map/ppermute | solution.py:28
  142.7 1.1 select_bitcast_fusion.1
  144.0 1.4 collective-permute-start.10
  145.4 7.5 %collective-permute-done.4 = bf16[256,1024]{1,0:T(8,128)(2,1)S(1)} collective-permute-done((bf16[256,1024]{1,0:T(8,128)(2,1)S(1)}, bf16[256,1024]{1,0:T(8,128)(2,1)S(1)}, u32[]{:S(2)}, u32[]{:S(2)}) %collective-permute-start.4) | collective-permute-done | bytes 524320 | tf_op jit(solution)/shard_map/ppermute | solution.py:28
  153.0 11.8 %all-to-all-start = ((bf16[64,128,256]{2,1,0:T(8,128)(2,1)}), bf16[64,128,256]{2,1,0:T(8,128)(2,1)}, u32[]{:S(2)}, u32[]{:S(2)}) async-start(bf16[64,128,256]{2,1,0:T(8,128)(2,1)} %collective-permute-done), calls=%async_computation | async-start | bytes 8388608 | tf_op jit(solution)/shard_map/all_to_all | solution.py:267
  165.0 2.7 collective-permute-start.6
  167.6 0.6 collective-permute-start.14
  168.3 1.1 slice_bitcast_fusion
  169.3 2.7 collective-permute-start.13
  172.0 1.1 slice_bitcast_fusion.1
  173.2 64.4 %collective-permute-done.6.refs_2_ = bf16[2,256,1024]{2,1,0:T(8,128)(2,1)S(1)} collective-permute-done((bf16[2,256,1024]{2,1,0:T(8,128)(2,1)S(1)}, bf16[2,256,1024]{2,1,0:T(8,128)(2,1)S(1)}, u32[]{:S(2)}, u32[]{:S(2)}) %collective-permute-start.6) | collective-permute-done | bytes 1048608 | tf_op jit(solution)/shard_map/ppermute | solution.py:28
  237.7 1.0 collective-permute-start.16
  238.7 0.3 copy-done.8
  239.0 1.0 copy-done.6
  240.0 0.9 collective-permute-start.15
  240.9 1.1 slice_bitcast_fusion.3
  242.0 1.6 collective-permute-start.7
  243.5 0.3 collective-permute-start.18
  243.8 6.5 %collective-permute-done.8.refs_4_ = bf16[256,1024]{1,0:T(8,128)(2,1)} collective-permute-done((bf16[256,1024]{1,0:T(8,128)(2,1)S(1)}, bf16[256,1024]{1,0:T(8,128)(2,1)}, u32[]{:S(2)}, u32[]{:S(2)}) %collective-permute-start.8) | collective-permute-done | bytes 524320 | tf_op jit(solution)/shard_map/ppermute | solution.py:28
  250.4 1.8 collective-permute-start.17
  252.2 1.4 copy.10.col_map_ref
  253.6 1.3 copy.11.col_map_ref
  254.9 0.6 stack.58.place_ref
  255.6 0.6 dynamic-slice_bitcast_fusion.3
  256.2 0.7 collective-permute-done.7.refs_3_
  256.9 0.7 copy-done.10
  257.6 0.2 copy-done.11
  258.0 0.4 copy-done.9
  258.4 17.8 %update.1.update_ref = f32[2,2,1024,1024]{3,2,1,0:T(8,128)} custom-call(s32[7]{0:T(128)} %stack.58.place_ref, bf16[2,256,1024]{2,1,0:T(8,128)(2,1)} %copy-done.4, bf16[2,256,1024]{2,1,0:T(8,128)(2,1)} %copy-done.6, bf16[2,256,1024]{2,1,0:T(8,128)(2,1)} %copy-done.5, bf16[256,1024]{1,0:T(8,128)(2,1)} %copy-done.10, ...), custom_call_target="tpu_custom_call" | custom-call | flops 8589934592 | bytes 29360128 | tf_op jit(solution)/shard_map/update/pallas_call | solution.py:118
  276.2 19.8 %place_first.1.base_ref = f32[1024,2048]{1,0:T(8,128)} custom-call(s32[7]{0:T(128)} %stack.58.place_ref, bf16[64,128,256]{2,1,0:T(8,128)(2,1)} %all-to-all-done.2.front_ref, f32[2,2,1024,1024]{3,2,1,0:T(8,128)} %update.1.update_ref, s32[1,1024]{1,0:T(1,128)} %get-tuple-element.17.row_map_ref, s32[2,1024,1]{2,1,0:T(8,128)} %copy.10.col_map_ref, ...), custom_call_target="tpu_custom_call" | custom-call | flops 8589934592 | bytes 29360128 | tf_op jit(solution)/shard_map/place_first/pallas_call | solution.py:197
  296.0 20.7 %place_last.1 = f32[1024,2048]{1,0:T(8,128)} custom-call(s32[7]{0:T(128)} %stack.58.place_ref, bf16[64,128,256]{2,1,0:T(8,128)(2,1)} %all-to-all-done.front_ref, f32[2,2,1024,1024]{3,2,1,0:T(8,128)} %update.1.update_ref, s32[1,1024]{1,0:T(1,128)} %get-tuple-element.18.row_map_ref, s32[2,1024,1]{2,1,0:T(8,128)} %copy.11.col_map_ref, ...), custom_call_target="tpu_custom_call" | custom-call | flops 8589934592 | bytes 29360128 | tf_op jit(solution)/shard_map/place_last/pallas_call | solution.py:197
  (56 shorter events, 1.3 us)
Async XLA Ops:
  0.0 1.0 copy-start
  3.4 30.6 %all-to-all-start.1 = ((bf16[8,768,128]{2,1,0:T(8,128)(2,1)}), bf16[8,768,128]{2,1,0:T(8,128)(2,1)S(1)}, u32[]{:S(2)}, u32[]{:S(2)}) async-start(bf16[8,768,128]{2,1,0:T(8,128)(2,1)} %pad_maximum_fusion), calls=%async_computation.1 | async-start | bytes 3145728 | tf_op jit(solution)/shard_map/all_to_all | solution.py:227
  27.4 125.6 %collective-permute-start = (bf16[64,128,256]{2,1,0:T(8,128)(2,1)}, bf16[64,128,256]{2,1,0:T(8,128)(2,1)}, u32[]{:S(2)}, u32[]{:S(2)}) collective-permute-start(bf16[64,128,256]{2,1,0:T(8,128)(2,1)} %bitcast.8), channel_id=1, source_target_pairs={{0,68},{1,69},{2,70},{3,71},{4,64},{5,65},{6,66},{7,67},{8,76},{9,... | collective-permute-start | bytes 12582920 | tf_op jit(solution)/shard_map/ppermute | solution.py:28
  34.0 119.0 %all-to-all-start.2 = ((bf16[64,128,256]{2,1,0:T(8,128)(2,1)}), bf16[64,128,256]{2,1,0:T(8,128)(2,1)}, u32[]{:S(2)}, u32[]{:S(2)}) async-start(bf16[64,128,256]{2,1,0:T(8,128)(2,1)} %bitcast.59), calls=%async_computation.2 | async-start | bytes 8388608 | tf_op jit(solution)/shard_map/all_to_all | solution.py:266
  43.1 3.0 copy-start.2
  43.1 3.0 collective-permute-start.1
  50.9 5.3 %collective-permute-start.2 = (bf16[128,1024]{1,0:T(8,128)(2,1)S(1)}, bf16[128,1024]{1,0:T(8,128)(2,1)S(1)}, u32[]{:S(2)}, u32[]{:S(2)}) collective-permute-start(bf16[128,1024]{1,0:T(8,128)(2,1)S(1)} %get-tuple-element.13), channel_id=1, source_target_pairs={{0,8},{1,24},{2,40},{3,56},{4,72},{5,88},{6,104},{7,120},{8,0},{9,... | collective-permute-start | bytes 786440 | tf_op jit(solution)/shard_map/ppermute | solution.py:28
  51.4 4.9 %collective-permute-start.3 = (bf16[128,1024]{1,0:T(8,128)(2,1)S(1)}, bf16[128,1024]{1,0:T(8,128)(2,1)S(1)}, u32[]{:S(2)}, u32[]{:S(2)}) collective-permute-start(bf16[128,1024]{1,0:T(8,128)(2,1)S(1)} %get-tuple-element.14), channel_id=1, source_target_pairs={{0,0},{1,16},{2,32},{3,48},{4,64},{5,80},{6,96},{7,112},{8,8},{9,2... | collective-permute-start | bytes 786440 | tf_op jit(solution)/shard_map/ppermute | solution.py:28
  52.1 90.6 %collective-permute-start.9 = (bf16[256,1024]{1,0:T(8,128)(2,1)}, bf16[256,1024]{1,0:T(8,128)(2,1)S(1)}, u32[]{:S(2)}, u32[]{:S(2)}) collective-permute-start(bf16[256,1024]{1,0:T(8,128)(2,1)} %lower.1), channel_id=1, source_target_pairs={{0,64},{1,65},{2,66},{3,67},{4,68},{5,69},{6,70},{7,71},{8,72},{9,... | collective-permute-start | bytes 1572872 | tf_op jit(solution)/shard_map/ppermute | solution.py:28
  56.4 96.5 %collective-permute-start.4 = (bf16[256,1024]{1,0:T(8,128)(2,1)S(1)}, bf16[256,1024]{1,0:T(8,128)(2,1)S(1)}, u32[]{:S(2)}, u32[]{:S(2)}) collective-permute-start(bf16[256,1024]{1,0:T(8,128)(2,1)S(1)} %bitcast.61), channel_id=1, source_target_pairs={{0,4},{1,5},{2,6},{3,7},{4,0},{5,1},{6,2},{7,3},{8,12},{9,13},{10,... | collective-permute-start | bytes 1572872 | tf_op jit(solution)/shard_map/ppermute | solution.py:28
  143.9 23.7 %copy-start.3 = (bf16[2,256,1024]{2,1,0:T(8,128)(2,1)}, bf16[2,256,1024]{2,1,0:T(8,128)(2,1)S(1)}, u32[]{:S(2)}) copy-start(bf16[2,256,1024]{2,1,0:T(8,128)(2,1)S(1)} %pad_maximum_fusion.2.refs_5_) | copy-start | bytes 3145732
  143.9 24.4 %collective-permute-start.11 = (bf16[2,256,1024]{2,1,0:T(8,128)(2,1)S(1)}, bf16[2,256,1024]{2,1,0:T(8,128)(2,1)}, u32[]{:S(2)}, u32[]{:S(2)}) collective-permute-start(bf16[2,256,1024]{2,1,0:T(8,128)(2,1)S(1)} %pad_maximum_fusion.2.refs_5_), channel_id=1, source_target_pairs={{0,48},{1,49},{2,50},{3,51},{4,52},{5,53},{6,54},{7,55},{8,56},{9,... | collective-permute-start | bytes 3145736 | tf_op jit(solution)/shard_map/ppermute | solution.py:28
  144.0 28.0 %collective-permute-start.10 = (bf16[2,256,1024]{2,1,0:T(8,128)(2,1)S(1)}, bf16[2,256,1024]{2,1,0:T(8,128)(2,1)}, u32[]{:S(2)}, u32[]{:S(2)}) collective-permute-start(bf16[2,256,1024]{2,1,0:T(8,128)(2,1)S(1)} %pad_maximum_fusion.2.refs_5_), channel_id=1, source_target_pairs={{0,16},{1,17},{2,18},{3,19},{4,20},{5,21},{6,22},{7,23},{8,24},{9,... | collective-permute-start | bytes 3145736 | tf_op jit(solution)/shard_map/ppermute | solution.py:28
  153.0 143.0 %all-to-all-start = ((bf16[64,128,256]{2,1,0:T(8,128)(2,1)}), bf16[64,128,256]{2,1,0:T(8,128)(2,1)}, u32[]{:S(2)}, u32[]{:S(2)}) async-start(bf16[64,128,256]{2,1,0:T(8,128)(2,1)} %collective-permute-done), calls=%async_computation | async-start | bytes 8388608 | tf_op jit(solution)/shard_map/all_to_all | solution.py:267
  164.8 76.0 %copy-start.7 = (s32[2,16384]{1,0:T(2,128)S(1)}, s32[2,16384]{1,0:T(2,128)}, u32[]{:S(2)}) copy-start(s32[2,16384]{1,0:T(2,128)} %param.8) | copy-start | bytes 393220
  164.9 72.8 %copy-start.4 = (bf16[2,256,1024]{2,1,0:T(8,128)(2,1)}, bf16[2,256,1024]{2,1,0:T(8,128)(2,1)S(1)}, u32[]{:S(2)}) copy-start(bf16[2,256,1024]{2,1,0:T(8,128)(2,1)S(1)} %pad_maximum_fusion.1.refs_0_) | copy-start | bytes 3145732
  165.0 72.6 %collective-permute-start.6 = (bf16[2,256,1024]{2,1,0:T(8,128)(2,1)S(1)}, bf16[2,256,1024]{2,1,0:T(8,128)(2,1)S(1)}, u32[]{:S(2)}, u32[]{:S(2)}) collective-permute-start(bf16[2,256,1024]{2,1,0:T(8,128)(2,1)S(1)} %pad_maximum_fusion.1.refs_0_), channel_id=1, source_target_pairs={{0,3},{1,0},{2,1},{3,2},{4,7},{5,4},{6,5},{7,6},{8,11},{9,8},{10,9... | collective-permute-start | bytes 3145736 | tf_op jit(solution)/shard_map/ppermute | solution.py:28
  167.6 70.1 %collective-permute-start.14 = (bf16[2,256,1024]{2,1,0:T(8,128)(2,1)S(1)}, bf16[2,256,1024]{2,1,0:T(8,128)(2,1)S(1)}, u32[]{:S(2)}, u32[]{:S(2)}) collective-permute-start(bf16[2,256,1024]{2,1,0:T(8,128)(2,1)S(1)} %pad_maximum_fusion.2.refs_5_), channel_id=1, source_target_pairs={{0,8},{1,9},{2,10},{3,11},{4,12},{5,13},{6,14},{7,15},{8,0},{9,1},... | collective-permute-start | bytes 3145736 | tf_op jit(solution)/shard_map/ppermute | solution.py:28
  168.3 70.4 %collective-permute-start.5 = (bf16[2,256,1024]{2,1,0:T(8,128)(2,1)S(1)}, bf16[2,256,1024]{2,1,0:T(8,128)(2,1)S(1)}, u32[]{:S(2)}, u32[]{:S(2)}) collective-permute-start(bf16[2,256,1024]{2,1,0:T(8,128)(2,1)S(1)} %pad_maximum_fusion.1.refs_0_), channel_id=1, source_target_pairs={{0,1},{1,2},{2,3},{3,0},{4,5},{5,6},{6,7},{7,4},{8,9},{9,10},{10,1... | collective-permute-start | bytes 3145736 | tf_op jit(solution)/shard_map/ppermute | solution.py:28
  169.3 72.6 %collective-permute-start.13 = (bf16[256,1024]{1,0:T(8,128)(2,1)S(1)}, bf16[256,1024]{1,0:T(8,128)(2,1)}, u32[]{:S(2)}, u32[]{:S(2)}) collective-permute-start(bf16[256,1024]{1,0:T(8,128)(2,1)S(1)} %slice_bitcast_fusion), channel_id=1, source_target_pairs={{0,48},{1,49},{2,50},{3,51},{4,52},{5,53},{6,54},{7,55},{8,56},{9,... | collective-permute-start | bytes 1572872 | tf_op jit(solution)/shard_map/ppermute | solution.py:28
  173.1 70.4 %collective-permute-start.12 = (bf16[256,1024]{1,0:T(8,128)(2,1)S(1)}, bf16[256,1024]{1,0:T(8,128)(2,1)}, u32[]{:S(2)}, u32[]{:S(2)}) collective-permute-start(bf16[256,1024]{1,0:T(8,128)(2,1)S(1)} %slice_bitcast_fusion.1), channel_id=1, source_target_pairs={{0,16},{1,17},{2,18},{3,19},{4,20},{5,21},{6,22},{7,23},{8,24},{9,... | collective-permute-start | bytes 1572872 | tf_op jit(solution)/shard_map/ppermute | solution.py:28
  237.6 1.1 copy-start.5
  237.6 12.7 %collective-permute-start.8 = (bf16[256,1024]{1,0:T(8,128)(2,1)S(1)}, bf16[256,1024]{1,0:T(8,128)(2,1)}, u32[]{:S(2)}, u32[]{:S(2)}) collective-permute-start(bf16[256,1024]{1,0:T(8,128)(2,1)S(1)} %slice_bitcast_fusion.2), channel_id=1, source_target_pairs={{0,3},{1,0},{2,1},{3,2},{4,7},{5,4},{6,5},{7,6},{8,11},{9,8},{10,9... | collective-permute-start | bytes 1572872 | tf_op jit(solution)/shard_map/ppermute | solution.py:28
  237.7 1.2 copy-start.8
  237.7 19.1 %collective-permute-start.16 = (bf16[2,256,1024]{2,1,0:T(8,128)(2,1)}, bf16[2,256,1024]{2,1,0:T(8,128)(2,1)S(1)}, u32[]{:S(2)}, u32[]{:S(2)}) collective-permute-start(bf16[2,256,1024]{2,1,0:T(8,128)(2,1)} %collective-permute-done.11.refs_7_), channel_id=1, source_target_pairs={{0,8},{1,9},{2,10},{3,11},{4,12},{5,13},{6,14},{7,15},{8,0},{9,1},... | collective-permute-start | bytes 3145736 | tf_op jit(solution)/shard_map/ppermute | solution.py:28
  239.0 1.0 copy-start.6
  240.0 16.9 %collective-permute-start.15 = (bf16[2,256,1024]{2,1,0:T(8,128)(2,1)}, bf16[2,256,1024]{2,1,0:T(8,128)(2,1)}, u32[]{:S(2)}, u32[]{:S(2)}) collective-permute-start(bf16[2,256,1024]{2,1,0:T(8,128)(2,1)} %collective-permute-done.10.refs_6_), channel_id=1, source_target_pairs={{0,8},{1,9},{2,10},{3,11},{4,12},{5,13},{6,14},{7,15},{8,0},{9,1},... | collective-permute-start | bytes 3145736 | tf_op jit(solution)/shard_map/ppermute | solution.py:28
  242.0 14.8 %collective-permute-start.7 = (bf16[256,1024]{1,0:T(8,128)(2,1)S(1)}, bf16[256,1024]{1,0:T(8,128)(2,1)S(1)}, u32[]{:S(2)}, u32[]{:S(2)}) collective-permute-start(bf16[256,1024]{1,0:T(8,128)(2,1)S(1)} %slice_bitcast_fusion.3), channel_id=1, source_target_pairs={{0,1},{1,2},{2,3},{3,0},{4,5},{5,6},{6,7},{7,4},{8,9},{9,10},{10,1... | collective-permute-start | bytes 1572872 | tf_op jit(solution)/shard_map/ppermute | solution.py:28
  243.5 13.3 %collective-permute-start.18 = (bf16[256,1024]{1,0:T(8,128)(2,1)}, bf16[256,1024]{1,0:T(8,128)(2,1)S(1)}, u32[]{:S(2)}, u32[]{:S(2)}) collective-permute-start(bf16[256,1024]{1,0:T(8,128)(2,1)} %collective-permute-done.13.refs_9_), channel_id=1, source_target_pairs={{0,8},{1,9},{2,10},{3,11},{4,12},{5,13},{6,14},{7,15},{8,0},{9,1},... | collective-permute-start | bytes 1572872 | tf_op jit(solution)/shard_map/ppermute | solution.py:28
  250.4 6.5 %collective-permute-start.17 = (bf16[256,1024]{1,0:T(8,128)(2,1)}, bf16[256,1024]{1,0:T(8,128)(2,1)S(1)}, u32[]{:S(2)}, u32[]{:S(2)}) collective-permute-start(bf16[256,1024]{1,0:T(8,128)(2,1)} %collective-permute-done.12.refs_8_), channel_id=1, source_target_pairs={{0,8},{1,9},{2,10},{3,11},{4,12},{5,13},{6,14},{7,15},{8,0},{9,1},... | collective-permute-start | bytes 1572872 | tf_op jit(solution)/shard_map/ppermute | solution.py:28
  256.8 0.8 copy-start.10
  256.8 1.0 copy-start.11
  256.8 1.1 copy-start.12
  256.9 1.5 copy-start.9
  296.0 20.7 %copy-start.1 = (bf16[1,1024,128]{2,1,0:T(8,128)(2,1)S(1)}, bf16[1,1024,128]{2,1,0:T(8,128)(2,1)}, u32[]{:S(2)}) copy-start(bf16[1,1024,128]{2,1,0:T(8,128)(2,1)} %param.7) | copy-start | bytes 786436
where the time goes:
time: 318 us; the launch traced here: 317 us
  starting transfers between devices  136 us (43%)
  waiting for transfers between devices  80.7 us (25%)
  Pallas kernels  62.1 us (20%)
  local copies, waits for them, and re-layouts  33.7 us (11%)
  other arithmetic  3.96 us (1%)
    ppermute x19, starting transfers between devices, shift(): return lax.ppermute(array, ALL, device_pairs(move))  109 us
    ppermute x19, waiting for transfers between devices, shift(): return lax.ppermute(array, ALL, device_pairs(move))  80.7 us
    pallas_call x2, Pallas kernels, place_child(): pl.pallas_call(functools.partial(place_kernel, flip, last), grid_spec=gri...  40.5 us
    unnamed x30, local copies, waits for them, and re-layouts  20.4 us
    pallas_call x1, Pallas kernels, update(): pl.pallas_call(update_kernel, grid=(2,), out_shape=jax.ShapeDtypeStruct((...  17.8 us
    all_to_all x1, starting transfers between devices, body(): arrived = lax.all_to_all(crossed, ('row', 'col'), 0, 0, tiled=True)  11.8 us
    all_to_all x1, starting transfers between devices, body(): stayed = lax.all_to_all(stay, ('row', 'col'), 0, 0, tiled=True)  8.97 us
    all_to_all x1, starting transfers between devices, body(): packet = lax.all_to_all(packet, 'col', 0, 0, tiled=True)  6.37 us
  transfers between devices with their start and end apart: 22, of which 5 were waited for; matrix products, arithmetic and copies ran while one was open for 10% of the time, Pallas kernels for 13%

commit v1 on v0

--- a/solution.py
+++ b/solution.py
@@ -28,12 +28,34 @@
     return lax.ppermute(array, ALL, device_pairs(move))
 
 
-def ring(array, forward, backward):
+def ring(array, forward, backward, beside=None):
     behind = shift(array, forward)
     ahead = shift(array, backward)
+    if beside is not None:
+        behind, ahead, _ = lax.optimization_barrier((behind, ahead, beside))
     far_first = shift(behind[0], forward)
     far_second = shift(ahead[1], backward)
     return array, behind, ahead, far_first, far_second
+
+
+def parcels_kernel(part_ref, front_ref, out_ref):
+    for c in range(8):
+        out_ref[c] = front_ref[:, c * 256 : (c + 1) * 256]
+
+
+def parcels(part, front):
+    return pl.pallas_call(
+        parcels_kernel,
+        grid_spec=pltpu.PrefetchScalarGridSpec(
+            num_scalar_prefetch=1,
+            grid=(8,),
+            in_specs=[pl.BlockSpec((128, 2048), lambda k, part: (part[0] * 8 + k, 0))],
+            out_specs=pl.BlockSpec((8, 128, 256), lambda k, part: (k, 0, 0)),
+        ),
+        out_shape=jax.ShapeDtypeStruct((64, 128, 256), BF16),
+        cost_estimate=pl.CostEstimate(flops=0, bytes_accessed=8 << 20, transcendentals=0),
+        name="parcels",
+    )(part.reshape(1), front)
 
 
 def lower_kernel(core_ref, panel_ref, mine_ref, other_ref, out_ref):
@@ -213,18 +235,22 @@
     x, core, zl, y = row // 2, row % 2, col // 4, col % 4
     target = half * 8 + row
 
-    parcels = front[0].reshape(2, 8, 128, 8, 256).transpose(0, 1, 3, 2, 4)
-    stay = lax.dynamic_index_in_dim(parcels, half, 0, keepdims=False).reshape(64, 128, 256)
-    leave = lax.dynamic_index_in_dim(parcels, 1 - half, 0, keepdims=False).reshape(
-        64, 128, 256
-    )
-    crossed = shift(leave, lambda zh, x, k, zl, y: (1 - zh, x, k, 1 - zl, y))
+    leave = parcels(1 - half, front[0])
+    stay = parcels(half, front[0])
+    crossed = [
+        shift(
+            leave[16 * part : 16 * part + 16],
+            lambda zh, x, k, zl, y: (1 - zh, x, k, 1 - zl, y),
+        )
+        for part in range(4)
+    ]
 
     inverse_share = lax.dynamic_slice_in_dim(inverse_block[0], core * 512, 512, 0)
     packet = jnp.concatenate(
         [panel[0].reshape(8, 256, 128), jnp.broadcast_to(inverse_share, (8, 512, 128))], 1
     )
     packet = lax.all_to_all(packet, "col", 0, 0, tiled=True)
+    packet, _ = lax.optimization_barrier((packet, crossed[0]))
     own_inverse = packet[:, 256:]
     other_inverse = shift(own_inverse, lambda zh, x, k, zl, y: (zh, x, 1 - k, zl, y))
     piece = lower_piece(core.reshape(1), packet[:, :256], own_inverse, other_inverse)
@@ -235,10 +261,12 @@
         )
 
     twin = shift(piece, lambda zh, x, k, zl, y: (1 - zh, x, k, zl, y))
+    pair, _ = lax.optimization_barrier((ordered(piece, twin, half == 1), crossed[1]))
     columns = ring(
-        ordered(piece, twin, half == 1),
+        pair,
         lambda zh, x, k, zl, y: (zh, (x + 1) % 4, k, zl, y),
         lambda zh, x, k, zl, y: (zh, (x + 3) % 4, k, zl, y),
+        crossed[2],
     )
     columns_other = [
         shift(part, lambda zh, x, k, zl, y: (zh, x, 1 - k, zl, y)) for part in columns
@@ -260,11 +288,15 @@
         lambda zh, x, k, zl, y: (zh, x, k, zl, (y + 3) % 4),
     )
 
+    stay, rows, columns, columns_other, _ = lax.optimization_barrier(
+        (stay, rows, columns, columns_other, crossed[3])
+    )
+    stayed = lax.all_to_all(stay, ("row", "col"), 0, 0, tiled=True)
+    crossed, stayed = lax.optimization_barrier((jnp.concatenate(crossed), stayed))
+    arrived = lax.all_to_all(crossed, ("row", "col"), 0, 0, tiled=True)
+
     place = jnp.stack([x, core, y, target, col, half, 1 - half]).astype(jnp.int32)
     updates = update(place, rows, columns, columns_other)
-
-    stayed = lax.all_to_all(stay, ("row", "col"), 0, 0, tiled=True)
-    arrived = lax.all_to_all(crossed, ("row", "col"), 0, 0, tiled=True)
 
     maps = child_maps.reshape(2, 8, 16, 128)
     row_maps = (

time: 318 us -> 313 us (0.984)
  starting transfers between devices: 136 us -> 94.9 us
  waiting for transfers between devices: 80.7 us -> 119 us
  local copies, waits for them, and re-layouts: 33.7 us -> 13.2 us
  Pallas kernels: 62.1 us -> 75.3 us
  other arithmetic: 3.96 us -> 7.46 us
    all_to_all x1, waiting for transfers between devices: 0.01 us -> 46.4 us  [body(): stayed = lax.all_to_all(stay, ('row', 'col'), 0, 0, tiled=True)]
    ppermute x19 -> x22, starting transfers between devices: 109 us -> 65.2 us  [shift(): return lax.ppermute(array, ALL, device_pairs(move))]
    unnamed x30 -> x31, local copies, waits for them, and re-layouts: 20.4 us -> 1.02 us
    ppermute x19 -> x22, waiting for transfers between devices: 80.7 us -> 64.6 us  [shift(): return lax.ppermute(array, ALL, device_pairs(move))]
    pallas_call x0 -> x2, Pallas kernels: none -> 13.2 us  [parcels(): pl.pallas_call(parcels_kernel, grid_spec=pltpu.PrefetchScalarGridSpec(num...]
    all_to_all x1, waiting for transfers between devices: 0.01 us -> 8.18 us  [body(): arrived = lax.all_to_all(crossed, ('row', 'col'), 0, 0, tiled=True)]
    all_to_all x1, starting transfers between devices: 8.97 us -> 15.4 us  [body(): stayed = lax.all_to_all(stay, ('row', 'col'), 0, 0, tiled=True)]
    another operation x1 -> x0, local copies, waits for them, and re-layouts: 4.01 us -> none
  transfers between devices with their start and end apart: 22 -> 25, of which waited for: 5 -> 10; matrix products, arithmetic and copies ran while one was open for 10% -> 5% of each run, Pallas kernels for 13% -> 16%
where the time goes in v1:
time: 313 us; the launch traced here: 310 us
  waiting for transfers between devices  119 us (38%)
  starting transfers between devices  94.9 us (30%)
  Pallas kernels  75.3 us (24%)
  local copies, waits for them, and re-layouts  13.2 us (4%)
  other arithmetic  7.46 us (2%)
    ppermute x22, starting transfers between devices, shift(): return lax.ppermute(array, ALL, device_pairs(move))  65.2 us
    ppermute x22, waiting for transfers between devices, shift(): return lax.ppermute(array, ALL, device_pairs(move))  64.6 us
    all_to_all x1, waiting for transfers between devices, body(): stayed = lax.all_to_all(stay, ('row', 'col'), 0, 0, tiled=True)  46.4 us
    pallas_call x2, Pallas kernels, place_child(): pl.pallas_call(functools.partial(place_kernel, flip, last), grid_spec=gri...  40.4 us
    pallas_call x1, Pallas kernels, update(): pl.pallas_call(update_kernel, grid=(2,), out_shape=jax.ShapeDtypeStruct((...  17.9 us
    all_to_all x1, starting transfers between devices, body(): stayed = lax.all_to_all(stay, ('row', 'col'), 0, 0, tiled=True)  15.4 us
    pallas_call x2, Pallas kernels, parcels(): pl.pallas_call(parcels_kernel, grid_spec=pltpu.PrefetchScalarGridSpec(num...  13.2 us
    all_to_all x1, waiting for transfers between devices, body(): arrived = lax.all_to_all(crossed, ('row', 'col'), 0, 0, tiled=True)  8.18 us
  transfers between devices with their start and end apart: 25, of which 10 were waited for; matrix products, arithmetic and copies ran while one was open for 5% of the time, Pallas kernels for 16%

profile of v1, /device:TPU:1, one launch (start us, length us, event | category | flops | bytes accessed | tf_op | source)
XLA Modules:
  0.0 310.4 jit_solution(6498324479831927574)
XLA Ops:
  0.0 0.9 copy-done
  1.1 2.3 pad_maximum_fusion.1
  3.5 6.4 %all-to-all-start = ((bf16[8,768,128]{2,1,0:T(8,128)(2,1)}), bf16[8,768,128]{2,1,0:T(8,128)(2,1)S(1)}, u32[]{:S(2)}, u32[]{:S(2)}) async-start(bf16[8,768,128]{2,1,0:T(8,128)(2,1)} %pad_maximum_fusion.1), calls=%async_computation | async-start | bytes 3145728 | tf_op jit(solution)/shard_map/all_to_all | solution.py:252
  9.8 6.6 %parcels.2 = bf16[64,128,256]{2,1,0:T(8,128)(2,1)} custom-call(s32[1]{0:T(128)} %bitcast.6.part_ref, bf16[2048,2048]{1,0:T(8,128)(2,1)} %bitcast.49), custom_call_target="tpu_custom_call" | custom-call | bytes 8388608 | tf_op jit(solution)/shard_map/parcels/pallas_call | solution.py:47
  16.4 4.0 %fusion = (bf16[16,128,256]{2,1,0:T(8,128)(2,1)S(1)}, bf16[16,128,256]{2,1,0:T(8,128)(2,1)}, bf16[16,128,256]{2,1,0:T(8,128)(2,1)}, bf16[16,128,256]{2,1,0:T(8,128)(2,1)}) fusion(bf16[64,128,256]{2,1,0:T(8,128)(2,1)} %parcels.2), kind=kLoop, calls=%fused_computation.25 | loop fusion | bytes 8388608 | tf_op jit(solution)/shard_map/slice | solution.py:242
  20.4 3.6 %collective-permute-start = (bf16[16,128,256]{2,1,0:T(8,128)(2,1)S(1)}, bf16[16,128,256]{2,1,0:T(8,128)(2,1)}, u32[]{:S(2)}, u32[]{:S(2)}) collective-permute-start(bf16[16,128,256]{2,1,0:T(8,128)(2,1)S(1)} %get-tuple-element.49), channel_id=1, source_target_pairs={{0,68},{1,69},{2,70},{3,71},{4,64},{5,65},{6,66},{7,67},{8,76},{9,... | collective-permute-start | bytes 3145736 | tf_op jit(solution)/shard_map/ppermute | solution.py:28
  24.0 22.4 %collective-permute-done = bf16[16,128,256]{2,1,0:T(8,128)(2,1)} collective-permute-done((bf16[16,128,256]{2,1,0:T(8,128)(2,1)S(1)}, bf16[16,128,256]{2,1,0:T(8,128)(2,1)}, u32[]{:S(2)}, u32[]{:S(2)}) %collective-permute-start) | collective-permute-done | bytes 1048608 | tf_op jit(solution)/shard_map/ppermute | solution.py:28
  46.4 1.9 collective-permute-start.4
  49.2 1.6 collective-permute-done.4.other_ref
  50.8 3.7 %lower.1 = bf16[256,1024]{1,0:T(8,128)(2,1)} custom-call(s32[1]{0:T(128)} %bitcast.1.core_ref, bf16[8,256,128]{2,1,0:T(8,128)(2,1)} %slice.34.panel_ref, bf16[8,512,128]{2,1,0:T(8,128)(2,1)} %copy-done.2, bf16[8,512,128]{2,1,0:T(8,128)(2,1)} %collective-permute-done.4.other_ref), custom_call_target="tpu_custom_call" | custom-call | flops 536870912 | bytes 3145728 | tf_op jit(solution)/shard_map/lower/pallas_call | solution.py:78
  54.5 1.1 constant_dynamic-slice_fusion.1
  56.7 2.8 collective-permute-start.1
  59.5 1.2 collective-permute-start.12
  60.7 2.0 collective-permute-start.2
  62.7 17.6 %collective-permute-start.7 = (bf16[256,1024]{1,0:T(8,128)(2,1)S(1)}, bf16[256,1024]{1,0:T(8,128)(2,1)S(1)}, u32[]{:S(2)}, u32[]{:S(2)}) collective-permute-start(bf16[256,1024]{1,0:T(8,128)(2,1)S(1)} %bitcast.51), channel_id=1, source_target_pairs={{0,4},{1,5},{2,6},{3,7},{4,0},{5,1},{6,2},{7,3},{8,12},{9,13},{10,... | collective-permute-start | bytes 1572872 | tf_op jit(solution)/shard_map/ppermute | solution.py:28
  80.4 1.1 select_bitcast_fusion.1
  81.6 12.5 %collective-permute-done.1 = bf16[16,128,256]{2,1,0:T(8,128)(2,1)S(1)} collective-permute-done((bf16[16,128,256]{2,1,0:T(8,128)(2,1)}, bf16[16,128,256]{2,1,0:T(8,128)(2,1)S(1)}, u32[]{:S(2)}, u32[]{:S(2)}) %collective-permute-start.1) | collective-permute-done | bytes 1048608 | tf_op jit(solution)/shard_map/ppermute | solution.py:28
  94.1 4.4 %collective-permute-start.13 = (bf16[2,256,1024]{2,1,0:T(8,128)(2,1)S(1)}, bf16[2,256,1024]{2,1,0:T(8,128)(2,1)}, u32[]{:S(2)}, u32[]{:S(2)}) collective-permute-start(bf16[2,256,1024]{2,1,0:T(8,128)(2,1)S(1)} %pad_maximum_fusion.3.refs_5_), channel_id=1, source_target_pairs={{0,16},{1,17},{2,18},{3,19},{4,20},{5,21},{6,22},{7,23},{8,24},{9,... | collective-permute-start | bytes 3145736 | tf_op jit(solution)/shard_map/ppermute | solution.py:28
  98.4 3.7 %collective-permute-start.14 = (bf16[2,256,1024]{2,1,0:T(8,128)(2,1)S(1)}, bf16[2,256,1024]{2,1,0:T(8,128)(2,1)}, u32[]{:S(2)}, u32[]{:S(2)}) collective-permute-start(bf16[2,256,1024]{2,1,0:T(8,128)(2,1)S(1)} %pad_maximum_fusion.3.refs_5_), channel_id=1, source_target_pairs={{0,48},{1,49},{2,50},{3,51},{4,52},{5,53},{6,54},{7,55},{8,56},{9,... | collective-permute-start | bytes 3145736 | tf_op jit(solution)/shard_map/ppermute | solution.py:28
  102.4 1.8 collective-permute-start.8
  104.2 3.1 collective-permute-start.3
  107.3 9.3 %collective-permute-done.2 = bf16[16,128,256]{2,1,0:T(8,128)(2,1)} collective-permute-done((bf16[16,128,256]{2,1,0:T(8,128)(2,1)}, bf16[16,128,256]{2,1,0:T(8,128)(2,1)}, u32[]{:S(2)}, u32[]{:S(2)}) %collective-permute-start.2) | collective-permute-done | bytes 1048608 | tf_op jit(solution)/shard_map/ppermute | solution.py:28
  116.6 1.5 collective-permute-start.17
  118.1 5.4 %collective-permute-done.13.refs_6_ = bf16[2,256,1024]{2,1,0:T(8,128)(2,1)} collective-permute-done((bf16[2,256,1024]{2,1,0:T(8,128)(2,1)S(1)}, bf16[2,256,1024]{2,1,0:T(8,128)(2,1)}, u32[]{:S(2)}, u32[]{:S(2)}) %collective-permute-start.13) | collective-permute-done | bytes 1048608 | tf_op jit(solution)/shard_map/ppermute | solution.py:28
  123.6 3.2 %collective-permute-start.9 = (bf16[2,256,1024]{2,1,0:T(8,128)(2,1)S(1)}, bf16[2,256,1024]{2,1,0:T(8,128)(2,1)S(1)}, u32[]{:S(2)}, u32[]{:S(2)}) collective-permute-start(bf16[2,256,1024]{2,1,0:T(8,128)(2,1)S(1)} %pad_maximum_fusion.2.refs_0_), channel_id=1, source_target_pairs={{0,3},{1,0},{2,1},{3,2},{4,7},{5,4},{6,5},{7,6},{8,11},{9,8},{10,9... | collective-permute-start | bytes 3145736 | tf_op jit(solution)/shard_map/ppermute | solution.py:28
  126.8 1.1 slice_bitcast_fusion.3
  127.8 1.9 collective-permute-start.15
  129.7 1.1 slice_bitcast_fusion.2
  130.8 0.9 collective-permute-start.16
  131.8 7.3 %collective-permute-done.3 = bf16[16,128,256]{2,1,0:T(8,128)(2,1)S(1)} collective-permute-done((bf16[16,128,256]{2,1,0:T(8,128)(2,1)S(1)}, bf16[16,128,256]{2,1,0:T(8,128)(2,1)S(1)}, u32[]{:S(2)}, u32[]{:S(2)}) %collective-permute-start.3) | collective-permute-done | bytes 1048608 | tf_op jit(solution)/shard_map/ppermute | solution.py:28
  139.1 4.2 %collective-permute-start.10 = (bf16[256,1024]{1,0:T(8,128)(2,1)S(1)}, bf16[256,1024]{1,0:T(8,128)(2,1)S(1)}, u32[]{:S(2)}, u32[]{:S(2)}) collective-permute-start(bf16[256,1024]{1,0:T(8,128)(2,1)S(1)} %slice_bitcast_fusion.1), channel_id=1, source_target_pairs={{0,1},{1,2},{2,3},{3,0},{4,5},{5,6},{6,7},{7,4},{8,9},{9,10},{10,1... | collective-permute-start | bytes 1572872 | tf_op jit(solution)/shard_map/ppermute | solution.py:28
  143.4 1.5 collective-permute-start.18
  144.9 2.1 collective-permute-done.9.refs_2_
  147.0 3.1 collective-permute-start.19
  150.2 3.5 %collective-permute-start.11 = (bf16[256,1024]{1,0:T(8,128)(2,1)S(1)}, bf16[256,1024]{1,0:T(8,128)(2,1)}, u32[]{:S(2)}, u32[]{:S(2)}) collective-permute-start(bf16[256,1024]{1,0:T(8,128)(2,1)S(1)} %slice_bitcast_fusion), channel_id=1, source_target_pairs={{0,3},{1,0},{2,1},{3,2},{4,7},{5,4},{6,5},{7,6},{8,11},{9,8},{10,9... | collective-permute-start | bytes 1572872 | tf_op jit(solution)/shard_map/ppermute | solution.py:28
  154.0 4.0 %collective-permute-done.10.refs_3_ = bf16[256,1024]{1,0:T(8,128)(2,1)S(1)} collective-permute-done((bf16[256,1024]{1,0:T(8,128)(2,1)S(1)}, bf16[256,1024]{1,0:T(8,128)(2,1)S(1)}, u32[]{:S(2)}, u32[]{:S(2)}) %collective-permute-start.10) | collective-permute-done | bytes 524320 | tf_op jit(solution)/shard_map/ppermute | solution.py:28
  158.0 1.9 collective-permute-start.21
  159.9 6.6 %parcels.3 = bf16[64,128,256]{2,1,0:T(8,128)(2,1)} custom-call(s32[1]{0:T(128)} %bitcast.5.part_ref, bf16[2048,2048]{1,0:T(8,128)(2,1)} %bitcast.50), custom_call_target="tpu_custom_call" | custom-call | bytes 8388608 | tf_op jit(solution)/shard_map/parcels/pallas_call | solution.py:47
  166.6 15.4 %all-to-all-start.1 = ((bf16[64,128,256]{2,1,0:T(8,128)(2,1)}), bf16[64,128,256]{2,1,0:T(8,128)(2,1)}, u32[]{:S(2)}, u32[]{:S(2)}) async-start(bf16[64,128,256]{2,1,0:T(8,128)(2,1)} %parcels.3), calls=%async_computation.1 | async-start | bytes 8388608 | tf_op jit(solution)/shard_map/all_to_all | solution.py:294
  182.1 3.5 %pad_maximum_fusion = bf16[64,128,256]{2,1,0:T(8,128)(2,1)} fusion(bf16[16,128,256]{2,1,0:T(8,128)(2,1)S(1)} %copy-done.9, bf16[16,128,256]{2,1,0:T(8,128)(2,1)} %collective-permute-done.2, bf16[16,128,256]{2,1,0:T(8,128)(2,1)S(1)} %copy-done.6, bf16[16,128,256]{2,1,0:T(8,128)(2,1)} %collective-permute-done), kind=kLoop, calls=%fused_computation | loop fusion | flops 6291456 | bytes 8388608 | tf_op jit(solution)/shard_map/concatenate | solution.py:295
  185.5 46.4 %all-to-all-done.1.front_ref = bf16[64,128,256]{2,1,0:T(8,128)(2,1)} async-done(((bf16[64,128,256]{2,1,0:T(8,128)(2,1)}), bf16[64,128,256]{2,1,0:T(8,128)(2,1)}, u32[]{:S(2)}, u32[]{:S(2)}) %all-to-all-start.1) | async-done | bytes 4194336 | tf_op jit(solution)/shard_map/all_to_all | solution.py:294
  231.9 7.9 %all-to-all-start.2 = ((bf16[64,128,256]{2,1,0:T(8,128)(2,1)}), bf16[64,128,256]{2,1,0:T(8,128)(2,1)}, u32[]{:S(2)}, u32[]{:S(2)}) async-start(bf16[64,128,256]{2,1,0:T(8,128)(2,1)} %pad_maximum_fusion), calls=%async_computation.2 | async-start | bytes 8388608 | tf_op jit(solution)/shard_map/all_to_all | solution.py:296
  240.1 1.4 copy.6.col_map_ref
  241.4 1.3 copy.7.col_map_ref
  244.0 17.9 %update.1.update_ref = f32[2,2,1024,1024]{3,2,1,0:T(8,128)} custom-call(s32[7]{0:T(128)} %stack.58.place_ref, bf16[2,256,1024]{2,1,0:T(8,128)(2,1)} %copy-done.4, bf16[2,256,1024]{2,1,0:T(8,128)(2,1)} %copy-done.10, bf16[2,256,1024]{2,1,0:T(8,128)(2,1)} %copy-done.11, bf16[256,1024]{1,0:T(8,128)(2,1)} %copy-done.14, ...), custom_call_target="tpu_custom_call" | custom-call | flops 8589934592 | bytes 29360128 | tf_op jit(solution)/shard_map/update/pallas_call | solution.py:140
  261.8 19.8 %place_first.1.base_ref = f32[1024,2048]{1,0:T(8,128)} custom-call(s32[7]{0:T(128)} %stack.58.place_ref, bf16[64,128,256]{2,1,0:T(8,128)(2,1)} %all-to-all-done.1.front_ref, f32[2,2,1024,1024]{3,2,1,0:T(8,128)} %update.1.update_ref, s32[1,1024]{1,0:T(1,128)} %get-tuple-element.63.row_map_ref, s32[2,1024,1]{2,1,0:T(8,128)} %copy.6.col_map_ref, ...), custom_call_target="tpu_custom_call" | custom-call | flops 8589934592 | bytes 29360128 | tf_op jit(solution)/shard_map/place_first/pallas_call | solution.py:219
  281.6 8.2 %all-to-all-done.2.front_ref = bf16[64,128,256]{2,1,0:T(8,128)(2,1)} async-done(((bf16[64,128,256]{2,1,0:T(8,128)(2,1)}), bf16[64,128,256]{2,1,0:T(8,128)(2,1)}, u32[]{:S(2)}, u32[]{:S(2)}) %all-to-all-start.2) | async-done | bytes 4194336 | tf_op jit(solution)/shard_map/all_to_all | solution.py:296
  289.8 20.7 %place_last.1 = f32[1024,2048]{1,0:T(8,128)} custom-call(s32[7]{0:T(128)} %stack.58.place_ref, bf16[64,128,256]{2,1,0:T(8,128)(2,1)} %all-to-all-done.2.front_ref, f32[2,2,1024,1024]{3,2,1,0:T(8,128)} %update.1.update_ref, s32[1,1024]{1,0:T(1,128)} %get-tuple-element.64.row_map_ref, s32[2,1024,1]{2,1,0:T(8,128)} %copy.7.col_map_ref, ...), custom_call_target="tpu_custom_call" | custom-call | flops 8589934592 | bytes 29360128 | tf_op jit(solution)/shard_map/place_last/pallas_call | solution.py:219
  (66 shorter events, 4.3 us)
Async XLA Ops:
  0.0 1.0 copy-start
  3.5 42.9 %all-to-all-start = ((bf16[8,768,128]{2,1,0:T(8,128)(2,1)}), bf16[8,768,128]{2,1,0:T(8,128)(2,1)S(1)}, u32[]{:S(2)}, u32[]{:S(2)}) async-start(bf16[8,768,128]{2,1,0:T(8,128)(2,1)} %pad_maximum_fusion.1), calls=%async_computation | async-start | bytes 3145728 | tf_op jit(solution)/shard_map/all_to_all | solution.py:252
  20.4 25.9 %collective-permute-start = (bf16[16,128,256]{2,1,0:T(8,128)(2,1)S(1)}, bf16[16,128,256]{2,1,0:T(8,128)(2,1)}, u32[]{:S(2)}, u32[]{:S(2)}) collective-permute-start(bf16[16,128,256]{2,1,0:T(8,128)(2,1)S(1)} %get-tuple-element.49), channel_id=1, source_target_pairs={{0,68},{1,69},{2,70},{3,71},{4,64},{5,65},{6,66},{7,67},{8,76},{9,... | collective-permute-start | bytes 3145736 | tf_op jit(solution)/shard_map/ppermute | solution.py:28
  46.4 4.4 %copy-start.2 = (bf16[8,512,128]{2,1,0:T(8,128)(2,1)}, bf16[8,512,128]{2,1,0:T(8,128)(2,1)S(1)}, u32[]{:S(2)}) copy-start(bf16[8,512,128]{2,1,0:T(8,128)(2,1)S(1)} %slice.35.mine_ref) | copy-start | bytes 3145732
  46.4 4.4 %collective-permute-start.4 = (bf16[8,512,128]{2,1,0:T(8,128)(2,1)S(1)}, bf16[8,512,128]{2,1,0:T(8,128)(2,1)}, u32[]{:S(2)}, u32[]{:S(2)}) collective-permute-start(bf16[8,512,128]{2,1,0:T(8,128)(2,1)S(1)} %slice.35.mine_ref), channel_id=1, source_target_pairs={{0,8},{1,9},{2,10},{3,11},{4,12},{5,13},{6,14},{7,15},{8,0},{9,1},... | collective-permute-start | bytes 3145736 | tf_op jit(solution)/shard_map/ppermute | solution.py:28
  55.6 7.1 %collective-permute-start.5 = (bf16[128,1024]{1,0:T(8,128)(2,1)S(1)}, bf16[128,1024]{1,0:T(8,128)(2,1)S(1)}, u32[]{:S(2)}, u32[]{:S(2)}) collective-permute-start(bf16[128,1024]{1,0:T(8,128)(2,1)S(1)} %get-tuple-element.59), channel_id=1, source_target_pairs={{0,8},{1,24},{2,40},{3,56},{4,72},{5,88},{6,104},{7,120},{8,0},{9,... | collective-permute-start | bytes 786440 | tf_op jit(solution)/shard_map/ppermute | solution.py:28
  56.0 6.6 %collective-permute-start.6 = (bf16[128,1024]{1,0:T(8,128)(2,1)S(1)}, bf16[128,1024]{1,0:T(8,128)(2,1)S(1)}, u32[]{:S(2)}, u32[]{:S(2)}) collective-permute-start(bf16[128,1024]{1,0:T(8,128)(2,1)S(1)} %get-tuple-element.60), channel_id=1, source_target_pairs={{0,0},{1,16},{2,32},{3,48},{4,64},{5,80},{6,96},{7,112},{8,8},{9,2... | collective-permute-start | bytes 786440 | tf_op jit(solution)/shard_map/ppermute | solution.py:28
  56.7 37.4 %collective-permute-start.1 = (bf16[16,128,256]{2,1,0:T(8,128)(2,1)}, bf16[16,128,256]{2,1,0:T(8,128)(2,1)S(1)}, u32[]{:S(2)}, u32[]{:S(2)}) collective-permute-start(bf16[16,128,256]{2,1,0:T(8,128)(2,1)} %get-tuple-element.52), channel_id=1, source_target_pairs={{0,68},{1,69},{2,70},{3,71},{4,64},{5,65},{6,66},{7,67},{8,76},{9,... | collective-permute-start | bytes 3145736 | tf_op jit(solution)/shard_map/ppermute | solution.py:28
  59.5 20.9 %collective-permute-start.12 = (bf16[256,1024]{1,0:T(8,128)(2,1)}, bf16[256,1024]{1,0:T(8,128)(2,1)S(1)}, u32[]{:S(2)}, u32[]{:S(2)}) collective-permute-start(bf16[256,1024]{1,0:T(8,128)(2,1)} %lower.1), channel_id=1, source_target_pairs={{0,64},{1,65},{2,66},{3,67},{4,68},{5,69},{6,70},{7,71},{8,72},{9,... | collective-permute-start | bytes 1572872 | tf_op jit(solution)/shard_map/ppermute | solution.py:28
  60.7 56.0 %collective-permute-start.2 = (bf16[16,128,256]{2,1,0:T(8,128)(2,1)}, bf16[16,128,256]{2,1,0:T(8,128)(2,1)}, u32[]{:S(2)}, u32[]{:S(2)}) collective-permute-start(bf16[16,128,256]{2,1,0:T(8,128)(2,1)} %get-tuple-element.51), channel_id=1, source_target_pairs={{0,68},{1,69},{2,70},{3,71},{4,64},{5,65},{6,66},{7,67},{8,76},{9,... | collective-permute-start | bytes 3145736 | tf_op jit(solution)/shard_map/ppermute | solution.py:28
  62.7 39.4 %collective-permute-start.7 = (bf16[256,1024]{1,0:T(8,128)(2,1)S(1)}, bf16[256,1024]{1,0:T(8,128)(2,1)S(1)}, u32[]{:S(2)}, u32[]{:S(2)}) collective-permute-start(bf16[256,1024]{1,0:T(8,128)(2,1)S(1)} %bitcast.51), channel_id=1, source_target_pairs={{0,4},{1,5},{2,6},{3,7},{4,0},{5,1},{6,2},{7,3},{8,12},{9,13},{10,... | collective-permute-start | bytes 1572872 | tf_op jit(solution)/shard_map/ppermute | solution.py:28
  81.6 68.6 %copy-start.3 = (bf16[2,256,1024]{2,1,0:T(8,128)(2,1)}, bf16[2,256,1024]{2,1,0:T(8,128)(2,1)S(1)}, u32[]{:S(2)}) copy-start(bf16[2,256,1024]{2,1,0:T(8,128)(2,1)S(1)} %pad_maximum_fusion.3.refs_5_) | copy-start | bytes 3145732
  94.1 8.2 %copy-start.5 = (bf16[16,128,256]{2,1,0:T(8,128)(2,1)}, bf16[16,128,256]{2,1,0:T(8,128)(2,1)S(1)}, u32[]{:S(2)}) copy-start(bf16[16,128,256]{2,1,0:T(8,128)(2,1)S(1)} %collective-permute-done.1) | copy-start | bytes 3145732
  94.1 29.5 %collective-permute-start.13 = (bf16[2,256,1024]{2,1,0:T(8,128)(2,1)S(1)}, bf16[2,256,1024]{2,1,0:T(8,128)(2,1)}, u32[]{:S(2)}, u32[]{:S(2)}) collective-permute-start(bf16[2,256,1024]{2,1,0:T(8,128)(2,1)S(1)} %pad_maximum_fusion.3.refs_5_), channel_id=1, source_target_pairs={{0,16},{1,17},{2,18},{3,19},{4,20},{5,21},{6,22},{7,23},{8,24},{9,... | collective-permute-start | bytes 3145736 | tf_op jit(solution)/shard_map/ppermute | solution.py:28
  98.4 28.3 %collective-permute-start.14 = (bf16[2,256,1024]{2,1,0:T(8,128)(2,1)S(1)}, bf16[2,256,1024]{2,1,0:T(8,128)(2,1)}, u32[]{:S(2)}, u32[]{:S(2)}) collective-permute-start(bf16[2,256,1024]{2,1,0:T(8,128)(2,1)S(1)} %pad_maximum_fusion.3.refs_5_), channel_id=1, source_target_pairs={{0,48},{1,49},{2,50},{3,51},{4,52},{5,53},{6,54},{7,55},{8,56},{9,... | collective-permute-start | bytes 3145736 | tf_op jit(solution)/shard_map/ppermute | solution.py:28
  102.1 2.1 copy-start.7
  102.4 64.1 %copy-start.4 = (bf16[2,256,1024]{2,1,0:T(8,128)(2,1)}, bf16[2,256,1024]{2,1,0:T(8,128)(2,1)S(1)}, u32[]{:S(2)}) copy-start(bf16[2,256,1024]{2,1,0:T(8,128)(2,1)S(1)} %pad_maximum_fusion.2.refs_0_) | copy-start | bytes 3145732
  102.4 28.4 %collective-permute-start.8 = (bf16[2,256,1024]{2,1,0:T(8,128)(2,1)S(1)}, bf16[2,256,1024]{2,1,0:T(8,128)(2,1)S(1)}, u32[]{:S(2)}, u32[]{:S(2)}) collective-permute-start(bf16[2,256,1024]{2,1,0:T(8,128)(2,1)S(1)} %pad_maximum_fusion.2.refs_0_), channel_id=1, source_target_pairs={{0,1},{1,2},{2,3},{3,0},{4,5},{5,6},{6,7},{7,4},{8,9},{9,10},{10,1... | collective-permute-start | bytes 3145736 | tf_op jit(solution)/shard_map/ppermute | solution.py:28
  104.2 34.9 %collective-permute-start.3 = (bf16[16,128,256]{2,1,0:T(8,128)(2,1)S(1)}, bf16[16,128,256]{2,1,0:T(8,128)(2,1)S(1)}, u32[]{:S(2)}, u32[]{:S(2)}) collective-permute-start(bf16[16,128,256]{2,1,0:T(8,128)(2,1)S(1)} %copy-done.7), channel_id=1, source_target_pairs={{0,68},{1,69},{2,70},{3,71},{4,64},{5,65},{6,66},{7,67},{8,76},{9,... | collective-permute-start | bytes 3145736 | tf_op jit(solution)/shard_map/ppermute | solution.py:28
  116.6 26.7 %collective-permute-start.17 = (bf16[2,256,1024]{2,1,0:T(8,128)(2,1)S(1)}, bf16[2,256,1024]{2,1,0:T(8,128)(2,1)S(1)}, u32[]{:S(2)}, u32[]{:S(2)}) collective-permute-start(bf16[2,256,1024]{2,1,0:T(8,128)(2,1)S(1)} %pad_maximum_fusion.3.refs_5_), channel_id=1, source_target_pairs={{0,8},{1,9},{2,10},{3,11},{4,12},{5,13},{6,14},{7,15},{8,0},{9,1},... | collective-permute-start | bytes 3145736 | tf_op jit(solution)/shard_map/ppermute | solution.py:28
  123.6 23.5 %collective-permute-start.9 = (bf16[2,256,1024]{2,1,0:T(8,128)(2,1)S(1)}, bf16[2,256,1024]{2,1,0:T(8,128)(2,1)S(1)}, u32[]{:S(2)}, u32[]{:S(2)}) collective-permute-start(bf16[2,256,1024]{2,1,0:T(8,128)(2,1)S(1)} %pad_maximum_fusion.2.refs_0_), channel_id=1, source_target_pairs={{0,3},{1,0},{2,1},{3,2},{4,7},{5,4},{6,5},{7,6},{8,11},{9,8},{10,9... | collective-permute-start | bytes 3145736 | tf_op jit(solution)/shard_map/ppermute | solution.py:28
  127.8 22.3 %collective-permute-start.15 = (bf16[256,1024]{1,0:T(8,128)(2,1)S(1)}, bf16[256,1024]{1,0:T(8,128)(2,1)}, u32[]{:S(2)}, u32[]{:S(2)}) collective-permute-start(bf16[256,1024]{1,0:T(8,128)(2,1)S(1)} %slice_bitcast_fusion.3), channel_id=1, source_target_pairs={{0,16},{1,17},{2,18},{3,19},{4,20},{5,21},{6,22},{7,23},{8,24},{9,... | collective-permute-start | bytes 1572872 | tf_op jit(solution)/shard_map/ppermute | solution.py:28
  130.8 27.2 %copy-start.10 = (bf16[2,256,1024]{2,1,0:T(8,128)(2,1)}, bf16[2,256,1024]{2,1,0:T(8,128)(2,1)S(1)}, u32[]{:S(2)}) copy-start(bf16[2,256,1024]{2,1,0:T(8,128)(2,1)S(1)} %collective-permute-done.8.refs_1_) | copy-start | bytes 3145732
  130.8 22.9 %collective-permute-start.16 = (bf16[256,1024]{1,0:T(8,128)(2,1)S(1)}, bf16[256,1024]{1,0:T(8,128)(2,1)}, u32[]{:S(2)}, u32[]{:S(2)}) collective-permute-start(bf16[256,1024]{1,0:T(8,128)(2,1)S(1)} %slice_bitcast_fusion.2), channel_id=1, source_target_pairs={{0,48},{1,49},{2,50},{3,51},{4,52},{5,53},{6,54},{7,55},{8,56},{9,... | collective-permute-start | bytes 1572872 | tf_op jit(solution)/shard_map/ppermute | solution.py:28
  139.1 11.1 %copy-start.8 = (bf16[16,128,256]{2,1,0:T(8,128)(2,1)}, bf16[16,128,256]{2,1,0:T(8,128)(2,1)S(1)}, u32[]{:S(2)}) copy-start(bf16[16,128,256]{2,1,0:T(8,128)(2,1)S(1)} %collective-permute-done.3) | copy-start | bytes 3145732
  139.1 18.8 %collective-permute-start.10 = (bf16[256,1024]{1,0:T(8,128)(2,1)S(1)}, bf16[256,1024]{1,0:T(8,128)(2,1)S(1)}, u32[]{:S(2)}, u32[]{:S(2)}) collective-permute-start(bf16[256,1024]{1,0:T(8,128)(2,1)S(1)} %slice_bitcast_fusion.1), channel_id=1, source_target_pairs={{0,1},{1,2},{2,3},{3,0},{4,5},{5,6},{6,7},{7,4},{8,9},{9,10},{10,1... | collective-permute-start | bytes 1572872 | tf_op jit(solution)/shard_map/ppermute | solution.py:28
  143.4 16.5 %copy-start.13 = (bf16[2,256,1024]{2,1,0:T(8,128)(2,1)}, bf16[2,256,1024]{2,1,0:T(8,128)(2,1)S(1)}, u32[]{:S(2)}) copy-start(bf16[2,256,1024]{2,1,0:T(8,128)(2,1)S(1)} %collective-permute-done.17.refs_10_) | copy-start | bytes 3145732
  143.4 23.2 %collective-permute-start.18 = (bf16[2,256,1024]{2,1,0:T(8,128)(2,1)}, bf16[2,256,1024]{2,1,0:T(8,128)(2,1)}, u32[]{:S(2)}, u32[]{:S(2)}) collective-permute-start(bf16[2,256,1024]{2,1,0:T(8,128)(2,1)} %collective-permute-done.13.refs_6_), channel_id=1, source_target_pairs={{0,8},{1,9},{2,10},{3,11},{4,12},{5,13},{6,14},{7,15},{8,0},{9,1},... | collective-permute-start | bytes 3145736 | tf_op jit(solution)/shard_map/ppermute | solution.py:28
  147.0 12.8 %copy-start.11 = (bf16[2,256,1024]{2,1,0:T(8,128)(2,1)}, bf16[2,256,1024]{2,1,0:T(8,128)(2,1)S(1)}, u32[]{:S(2)}) copy-start(bf16[2,256,1024]{2,1,0:T(8,128)(2,1)S(1)} %collective-permute-done.9.refs_2_) | copy-start | bytes 3145732
  147.0 19.5 %collective-permute-start.19 = (bf16[2,256,1024]{2,1,0:T(8,128)(2,1)}, bf16[2,256,1024]{2,1,0:T(8,128)(2,1)}, u32[]{:S(2)}, u32[]{:S(2)}) collective-permute-start(bf16[2,256,1024]{2,1,0:T(8,128)(2,1)} %collective-permute-done.14.refs_7_), channel_id=1, source_target_pairs={{0,8},{1,9},{2,10},{3,11},{4,12},{5,13},{6,14},{7,15},{8,0},{9,1},... | collective-permute-start | bytes 3145736 | tf_op jit(solution)/shard_map/ppermute | solution.py:28
  150.2 16.3 %collective-permute-start.11 = (bf16[256,1024]{1,0:T(8,128)(2,1)S(1)}, bf16[256,1024]{1,0:T(8,128)(2,1)}, u32[]{:S(2)}, u32[]{:S(2)}) collective-permute-start(bf16[256,1024]{1,0:T(8,128)(2,1)S(1)} %slice_bitcast_fusion), channel_id=1, source_target_pairs={{0,3},{1,0},{2,1},{3,2},{4,7},{5,4},{6,5},{7,6},{8,11},{9,8},{10,9... | collective-permute-start | bytes 1572872 | tf_op jit(solution)/shard_map/ppermute | solution.py:28
  153.7 12.8 %collective-permute-start.20 = (bf16[256,1024]{1,0:T(8,128)(2,1)}, bf16[256,1024]{1,0:T(8,128)(2,1)}, u32[]{:S(2)}, u32[]{:S(2)}) collective-permute-start(bf16[256,1024]{1,0:T(8,128)(2,1)} %collective-permute-done.15.refs_8_), channel_id=1, source_target_pairs={{0,8},{1,9},{2,10},{3,11},{4,12},{5,13},{6,14},{7,15},{8,0},{9,1},... | collective-permute-start | bytes 1572872 | tf_op jit(solution)/shard_map/ppermute | solution.py:28
  158.0 1.9 copy-start.14
  158.0 8.6 %collective-permute-start.21 = (bf16[256,1024]{1,0:T(8,128)(2,1)}, bf16[256,1024]{1,0:T(8,128)(2,1)}, u32[]{:S(2)}, u32[]{:S(2)}) collective-permute-start(bf16[256,1024]{1,0:T(8,128)(2,1)} %collective-permute-done.16.refs_9_), channel_id=1, source_target_pairs={{0,8},{1,9},{2,10},{3,11},{4,12},{5,13},{6,14},{7,15},{8,0},{9,1},... | collective-permute-start | bytes 1572872 | tf_op jit(solution)/shard_map/ppermute | solution.py:28
  166.5 15.5 %copy-start.6 = (bf16[16,128,256]{2,1,0:T(8,128)(2,1)S(1)}, bf16[16,128,256]{2,1,0:T(8,128)(2,1)}, u32[]{:S(2)}) copy-start(bf16[16,128,256]{2,1,0:T(8,128)(2,1)} %copy-done.5) | copy-start | bytes 3145732
  166.5 15.5 %copy-start.9 = (bf16[16,128,256]{2,1,0:T(8,128)(2,1)S(1)}, bf16[16,128,256]{2,1,0:T(8,128)(2,1)}, u32[]{:S(2)}) copy-start(bf16[16,128,256]{2,1,0:T(8,128)(2,1)} %copy-done.8) | copy-start | bytes 3145732
  166.6 65.4 %all-to-all-start.1 = ((bf16[64,128,256]{2,1,0:T(8,128)(2,1)}), bf16[64,128,256]{2,1,0:T(8,128)(2,1)}, u32[]{:S(2)}, u32[]{:S(2)}) async-start(bf16[64,128,256]{2,1,0:T(8,128)(2,1)} %parcels.3), calls=%async_computation.1 | async-start | bytes 8388608 | tf_op jit(solution)/shard_map/all_to_all | solution.py:294
  185.5 54.3 %copy-start.12 = (s32[2,16384]{1,0:T(2,128)S(1)}, s32[2,16384]{1,0:T(2,128)}, u32[]{:S(2)}) copy-start(s32[2,16384]{1,0:T(2,128)} %param.8) | copy-start | bytes 393220
  231.9 57.8 %all-to-all-start.2 = ((bf16[64,128,256]{2,1,0:T(8,128)(2,1)}), bf16[64,128,256]{2,1,0:T(8,128)(2,1)}, u32[]{:S(2)}, u32[]{:S(2)}) async-start(bf16[64,128,256]{2,1,0:T(8,128)(2,1)} %pad_maximum_fusion), calls=%async_computation.2 | async-start | bytes 8388608 | tf_op jit(solution)/shard_map/all_to_all | solution.py:296
  289.8 20.7 %copy-start.1 = (bf16[1,1024,128]{2,1,0:T(8,128)(2,1)S(1)}, bf16[1,1024,128]{2,1,0:T(8,128)(2,1)}, u32[]{:S(2)}) copy-start(bf16[1,1024,128]{2,1,0:T(8,128)(2,1)} %param.7) | copy-start | bytes 786436
